TPU v7x, 128 devices: a whole 4x4x4 slice. The times are simulated.
128 devices in a mesh: row: 16 (over z, y_hi, core), col: 8 (over y_lo, x).
Axes of the slice: x: 4, y: 4 (y_hi: 2, y_lo: 2; y = y_hi * 2 + y_lo), z: 4, core: 2. Of those that a mesh axis runs over, the one named last changes fastest.
Arguments:
- activations: bfloat16 [2048, 8192], P('col', 'row'), may hold values from -0.13183594 to 0.13183594
- out_grad: bfloat16 [2048, 28672], P('row', 'col'), may hold values from -6 to 6
- weight: bfloat16 [8192, 28672], P('row', 'col'), may hold values from -0.0625 to 0.0625
- block_mask: int32 [128, 448], P('row', 'col'), may hold values from 0 to 1, as said below
Outputs:
- weight_grad: float32 [8192, 28672], P('row', 'col')
- input_grad: bfloat16 [2048, 8192], P('col', 'row')
Inputs may be any that keep to these rules, and one draw needn't show every extreme that they name: `block_mask`: taken in tiles of 8 x 56 blocks (the blocks of one device), each tile holds at most 224 nonzero entries, and some tile holds exactly 224.
All inputs are finite; a program needn't handle non-finite values.
Results may differ from a plain program's by a relative error of at most 0.017.
Values may be sent and summed in bfloat16 or wider, within the bound.
A program may use at most 128 MiB of HBM per device.

v0:
```python
import jax
import jax.numpy as jnp
from jax import lax
from jax.sharding import PartitionSpec as P

BLK = 64


def local(activations, out_grad, weight, block_mask):
    x_full = lax.all_gather(activations, "col", axis=0, tiled=True)
    cols_loc = weight.shape[1]
    nbc = cols_loc // BLK
    spread = (
        lax.broadcasted_iota(jnp.int32, (nbc, cols_loc), 1) // BLK
        == lax.broadcasted_iota(jnp.int32, (nbc, cols_loc), 0)
    ).astype(jnp.bfloat16)
    mask_cols = jnp.dot(block_mask.astype(jnp.bfloat16), spread, preferred_element_type=jnp.float32)
    mask_full = jnp.repeat(mask_cols, BLK, axis=0)
    masked_w = weight * mask_full.astype(jnp.bfloat16)
    dy_full = lax.all_gather(out_grad, "row", axis=0, tiled=True)
    grad_part = lax.dot_general(
        x_full, dy_full, (((0,), (0,)), ((), ())), preferred_element_type=jnp.float32
    )
    dx_part = lax.dot_general(
        dy_full, masked_w, (((1,), (1,)), ((), ())), preferred_element_type=jnp.float32
    )
    weight_grad = grad_part * mask_full
    partial_rounded = dx_part.astype(jnp.bfloat16)
    input_grad = lax.psum_scatter(partial_rounded, "col", scatter_dimension=0, tiled=True).astype(
        jnp.float32
    )
    return (weight_grad, input_grad.astype(jnp.bfloat16))


def solution(mesh):
    in_specs = (P("col", "row"), P("row", "col"), P("row", "col"), P("row", "col"))
    out_specs = (P("row", "col"), P("col", "row"))
    return jax.shard_map(local, mesh=mesh, in_specs=in_specs, out_specs=out_specs, check_vma=False)
```

profile of v0, /device:TPU:0, one launch (start us, length us, event | category | flops | bytes accessed | tf_op | source)
XLA Modules:
  0.0 206.1 jit_solution(15646260499582229720)
XLA Ops:
  7.2 0.0 all-gather.5.cloned.1.call-start
  7.2 0.7 all-gather.5.cloned.1.call-update
  7.9 0.0 all-gather.3.cloned.1.call-start
  7.9 0.7 all-gather.3.cloned.1.call-update
  8.6 0.0 reduce-scatter.2.cloned.1.call-start
  8.7 0.9 convolution_bitcast_fusion
  9.7 4.1 %fusion = bf16[512,3584]{1,0:T(8,128)(2,1)} fusion(bf16[512,3584]{1,0:T(8,128)(2,1)} %param.6, f32[8,3584]{1,0:T(8,128)S(1)} %convolution_bitcast_fusion), kind=kLoop, calls=%fused_computation.3 | loop fusion | flops 1835008 | bytes 7454720 | tf_op jit(solution)/shard_map/mul | solution.py:19
  13.8 99.0 %all-gather.5.cloned.1.call-done = bf16[2048,3584]{1,0:T(8,128)(2,1)} async-done(((bf16[128,3584]{1,0:T(8,128)(2,1)}), bf16[2048,3584]{1,0:T(8,128)(2,1)}) %all-gather.5.cloned.1.call-update) | async-done | bytes 14680080 | tf_op jit(solution)/shard_map/all_gather | solution.py:20
  112.8 13.1 %fusion.1 = bf16[2048,512]{0,1:T(8,128)(2,1)} fusion(bf16[512,3584]{1,0:T(8,128)(2,1)} %fusion, bf16[2048,3584]{1,0:T(8,128)(2,1)} %all-gather.5.cloned.1.call-done), kind=kOutput, calls=%fused_computation.5 | convolution fusion | flops 7517241344 | bytes 20447232 | tf_op jit(solution)/shard_map/dot_general | solution.py:24
  125.9 0.0 reduce-scatter.2.cloned.1.call-update
  125.9 27.4 %all-gather.3.cloned.1.call-done = bf16[2048,512]{1,0:T(8,128)(2,1)} async-done(((bf16[256,512]{1,0:T(8,128)(2,1)}), bf16[2048,512]{1,0:T(8,128)(2,1)}) %all-gather.3.cloned.1.call-update) | async-done | bytes 2097168 | tf_op jit(solution)/shard_map/all_gather | solution.py:10
  153.4 13.6 %bitcast_multiply_fusion = f32[512,3584]{1,0:T(8,128)} fusion(bf16[2048,512]{1,0:T(8,128)(2,1)} %all-gather.3.cloned.1.call-done, bf16[2048,3584]{1,0:T(8,128)(2,1)} %all-gather.5.cloned.1.call-done, f32[8,3584]{1,0:T(8,128)S(1)} %convolution_bitcast_fusion), kind=kOutput, calls=%fused_computation.1 | convolution fusion | flops 7518027776 | bytes 24231936 | tf_op jit(solution)/shard_map/dot_general | solution.py:21
  167.0 30.8 %reduce-scatter.2.cloned.1.call-done = bf16[256,512]{0,1:T(8,128)(2,1)} async-done(((bf16[2048,512]{0,1:T(8,128)(2,1)}), bf16[256,512]{0,1:T(8,128)(2,1)}) %reduce-scatter.2.cloned.1.call-update) | async-done | bytes 262160 | tf_op jit(solution)/shard_map/reduce_scatter | solution.py:29
  197.8 1.8 copy.6
  (2 shorter events, 0.0 us)
Async XLA Ops:
  7.2 105.6 %all-gather.5.cloned.1.call-start = ((), (), s32[]{:S(2)}) async-start(), calls=%async_computation.2 | async-start | bytes 15597568 | tf_op jit(solution)/shard_map/all_gather | solution.py:20
  7.9 145.5 %all-gather.3.cloned.1.call-start = ((), (), s32[]{:S(2)}) async-start(), calls=%async_computation.1 | async-start | bytes 2359296 | tf_op jit(solution)/shard_map/all_gather | solution.py:10
  8.6 189.1 %reduce-scatter.2.cloned.1.call-start = ((), (), s32[]{:S(2)}) async-start(), calls=%async_computation.3 | async-start | bytes 2359296 | tf_op jit(solution)/shard_map/reduce_scatter | solution.py:29
Sparse Core Ops, SparseCore 0:
  10.5 102.2 all-gather.4
  114.4 38.8 all-gather.2
  155.8 41.9 reduce-scatter.1
where the time goes:
time: 206 us
  waiting for transfers between devices  159 us (77%)
  matrix products  27.7 us (13%)
  between operations  13.8 us (7%)
  other arithmetic  4.16 us (2%)
    all_gather x1, waiting for transfers between devices, local(): dy_full = lax.all_gather(out_grad, 'row', axis=0, tiled=True)  99 us
    reduce_scatter x1, waiting for transfers between devices, local(): lax.psum_scatter(partial_rounded, 'col', scatter_dimension=0, tiled=True)  30.8 us
    all_gather x1, waiting for transfers between devices, local(): x_full = lax.all_gather(activations, 'col', axis=0, tiled=True)  27.4 us
    dot_general x1, matrix products, local(): lax.dot_general(x_full, dy_full, (((0,), (0,)), ((), ())), preferred_elem...  13.6 us
    dot_general x1, matrix products, local(): lax.dot_general(dy_full, masked_w, (((1,), (1,)), ((), ())), preferred_el...  13.1 us
    mul x1, other arithmetic, local(): masked_w = weight * mask_full.astype(jnp.bfloat16)  4.14 us
  transfers between devices with their start and end apart: 3, of which 3 were waited for; matrix products, arithmetic and copies ran while one was open for 15% of the time, Pallas kernels for 0%

commit v1 on v0

v1 whole, which is shorter than its diff:
```python
import functools

import jax
import jax.numpy as jnp
from jax import lax
from jax.experimental import pallas as pl
from jax.experimental.pallas import tpu as pltpu
from jax.sharding import PartitionSpec as P

BLK = 64
STEPS = 8
ROWS = 16
AHEAD = 3
MESH = pl.DeviceIdType.MESH

M1, OWN, P1, Z2, Y, YP1, YZ2, YM1 = range(8)
S_ZP, S_ZM, S_Y, S_FWD, S_YZP, S_YZM, S_Y2 = range(7)


def slot_of(dz, dh):
    return 4 * dh + (dz + 1 - dh) % 4


def comm_kernel(
    x_ref, dy_ref, w_ref, mask_ref,
    acc_ref, ig_ref,
    dyf, xp, xt, wv, wmt, mcols, dxb, rsb, ysend, yland,
    s_piece, r_piece, s_core, r_core, s_x, r_x, s_rs, r_rs, s_y, r_y, loc,
):
    row, col = lax.axis_index("row"), lax.axis_index("col")
    core = lax.rem(row, 2)
    h = lax.rem(lax.div(row, 2), 2)
    z = lax.div(row, 4)
    x = lax.rem(col, 4)
    yl = lax.div(col, 4)

    def row_id(z_, h_, c_):
        return (z_ * 2 + h_) * 2 + c_

    zp = (row_id(lax.rem(z + 1, 4), h, core), col)
    zm = (row_id(lax.rem(z + 3, 4), h, core), col)
    yp = (row_id(z, 1 - h, core), col)
    other_core = (row_id(z, h, 1 - core), col)
    yn = (row, (1 - yl) * 4 + x)

    def xpeer(o):
        return (row, yl * 4 + lax.rem(x + o, 4))

    barrier = pltpu.get_barrier_semaphore()
    partners = [zp, zm, yp, other_core, yn, xpeer(1), xpeer(2), xpeer(3)]
    for dev in partners:
        pl.semaphore_signal(barrier, inc=1, device_id=dev, device_id_type=MESH)

    own_dy = pltpu.make_async_copy(dy_ref, dyf.at[:, core, OWN], loc.at[0])
    own_dy.start()
    w_copy = pltpu.make_async_copy(w_ref, wv, loc.at[1])
    w_copy.start()

    def x_slot(yl_):
        j = yl_ * 4 + x
        dz = lax.rem(lax.div(j, 2) + 4 - z, 4)
        dh = lax.rem(lax.rem(j, 2) + 2 - h, 2)
        return 4 * dh + lax.rem(dz + 5 - dh, 4)

    own_x = [pltpu.make_async_copy(x_ref.at[c], xp.at[:, c, x_slot(yl)], loc.at[2 + c]) for c in range(2)]
    for cp in own_x:
        cp.start()

    pl.semaphore_wait(barrier, len(partners))

    def remote(src, dst, ss, rs, dev):
        return pltpu.make_async_remote_copy(
            src_ref=src, dst_ref=dst, send_sem=ss, recv_sem=rs, device_id=dev, device_id_type=MESH
        )

    def piece(kind, p):
        src_slot, dst_slot, dev = {
            S_ZP: (None, M1, zp),
            S_ZM: (None, P1, zm),
            S_Y: (None, Y, yp),
            S_YZP: (Y, YM1, zp),
            S_YZM: (Y, YP1, zm),
            S_Y2: (Z2, YZ2, yp),
        }[kind]
        src = dy_ref.at[p] if src_slot is None else dyf.at[p, core, src_slot]
        return remote(src, dyf.at[p, core, dst_slot], s_piece.at[kind, p], r_piece.at[dst_slot, p], dev)

    def fwd(p, up):
        src = dyf.at[p, core, M1 if up else P1]
        return remote(src, dyf.at[p, core, Z2], s_piece.at[S_FWD, p], r_piece.at[Z2, p], zp if up else zm)

    def to_core(g, p):
        lo, n = ((0, 3), (3, 5))[g]
        there = dyf.at[p, core, pl.ds(lo, n)]
        return remote(there, there, s_core.at[g, p], r_core.at[g, p], other_core)

    def from_core(g, p):
        lo, n = ((0, 3), (3, 5))[g]
        here = dyf.at[p, 1 - core, pl.ds(lo, n)]
        return remote(here, here, s_core.at[g, p], r_core.at[g, p], other_core)

    def own_sends(p):
        for kind in (S_ZP, S_ZM, S_Y):
            piece(kind, p).start()

    def x_send(o, c):
        there = xp.at[:, c, x_slot(yl)]
        return remote(x_ref.at[c], there, s_x.at[0, o, c], r_x.at[0, o, c], xpeer(o) if o else yn)

    def x_hand(o, c):
        there = xp.at[:, c, x_slot(1 - yl)]
        return remote(there, there, s_x.at[1, o, c], r_x.at[1, o, c], xpeer(o))

    dzp_own = lax.rem(lax.div(x, 2) + 4 - z, 2)
    dh_own = lax.rem(lax.rem(x, 2) + 2 - h, 2)
    cls_own = dh_own * 2 + dzp_own
    keep = lax.rem(yl + lax.div(lax.rem(z + dzp_own, 4), 2), 2)

    def cls_dest(cls):
        dh, dzp = cls // 2, cls % 2
        return 2 * lax.rem(z + dzp, 2) + lax.rem(h + dh, 2)

    def rs_send(cls, p):
        xs = cls_dest(cls)
        o = lax.rem(x + 4 - xs + 3, 4)
        return remote(dxb.at[p, cls], rsb.at[o, p], s_rs.at[cls, p], r_rs.at[o, p], (row, yl * 4 + xs))

    def rs_recv(o, p):
        return remote(rsb.at[o, p], rsb.at[o, p], s_rs.at[0, p], r_rs.at[o, p], xpeer(1))

    def y_send(p):
        return remote(ysend.at[p], yland.at[p], s_y.at[p], r_y.at[p], yn)

    for p in range(AHEAD):
        own_sends(p)
    for c in range(2):
        for o in range(4):
            x_send(o, c).start()

    d_loc, f_loc = wv.shape
    nbr, nbc = mask_ref.shape
    tile = 512
    n_tiles = f_loc // tile
    mask_bf = mask_ref[...].astype(jnp.bfloat16)

    def spread(i, _):
        cols = pl.ds(pl.multiple_of(i * tile, tile), tile)
        block = lax.broadcasted_iota(jnp.int32, (nbc, tile), 0)
        first = block * BLK - i * tile
        lane = lax.broadcasted_iota(jnp.int32, (nbc, tile), 1)
        hit = jnp.logical_and(lane >= first, lane < first + BLK)
        pick = jnp.where(hit, 1.0, 0.0).astype(jnp.bfloat16)
        mcols[:, cols] = jnp.dot(mask_bf, pick, preferred_element_type=jnp.float32)
        return 0

    lax.fori_loop(0, n_tiles, spread, 0)
    w_copy.wait()

    def mask_w(i, _):
        cols = pl.ds(pl.multiple_of(i * tile, tile), tile)
        upper = lax.broadcasted_iota(jnp.int32, (2 * BLK, tile), 0) < BLK
        for b in range(d_loc // (2 * BLK)):
            m = jnp.where(upper, mcols[2 * b : 2 * b + 1, cols], mcols[2 * b + 1 : 2 * b + 2, cols])
            wm = wv[b * 2 * BLK : (b + 1) * 2 * BLK, cols] * m.astype(jnp.bfloat16)
            wmt[cols, b * 2 * BLK : (b + 1) * 2 * BLK] = wm.T
        return 0

    lax.fori_loop(0, n_tiles, mask_w, 0)
    own_dy.wait()

    def wgrad(b, first, last):
        span = xt.shape[1]
        xt[...] = xp[pl.ds(2 * b, 2)].reshape(span, d_loc).T

        def one(i, _):
            cols = pl.ds(pl.multiple_of(i * tile, tile), tile)
            dy2 = dyf[pl.ds(2 * b, 2), :, :, :, cols].reshape(span, tile)
            part = jnp.dot(xt[...], dy2, preferred_element_type=jnp.float32)
            if not first:
                part = part + acc_ref[:, cols]
            if last:
                for i_b in range(nbr):
                    rows = slice(i_b * BLK, (i_b + 1) * BLK)
                    acc_ref[rows, cols] = part[rows] * mcols[i_b : i_b + 1, cols]
            else:
                acc_ref[:, cols] = part
            return 0

        lax.fori_loop(0, n_tiles, one, 0)

    def in_range(s, lag):
        return jnp.logical_and(s >= lag, s < STEPS + lag)

    def step(s, _):
        @pl.when(s < STEPS)
        def _():
            piece(S_ZP, s).wait_recv()
            piece(S_ZM, s).wait_recv()

            @pl.when(s < STEPS - AHEAD)
            def _():
                own_sends(s + AHEAD)

            @pl.when(lax.rem(s, 2) == 0)
            def _():
                fwd(s, True).start()

            @pl.when(lax.rem(s, 2) == 1)
            def _():
                fwd(s, False).start()

            to_core(0, s).start()
            piece(S_Y, s).wait_recv()
            piece(S_YZP, s).start()
            piece(S_YZM, s).start()

        @pl.when(s == 0)
        def _():
            for c in range(2):
                x_send(0, c).wait_recv()
                for o in range(1, 4):
                    x_hand(o, c).start()

        @pl.when(in_range(s, 1))
        def _():
            q = s - 1
            fwd(q, True).wait_recv()
            piece(S_Y2, q).start()
            piece(S_YZP, q).wait_recv()
            piece(S_YZM, q).wait_recv()

        @pl.when(in_range(s, 2))
        def _():
            q = s - 2
            piece(S_Y2, q).wait_recv()
            to_core(1, q).start()

        @pl.when(in_range(s, 3))
        def _():
            q = s - 3
            from_core(0, q).wait_recv()
            from_core(1, q).wait_recv()
            part = jnp.dot(
                dyf[q].reshape(16 * ROWS, f_loc), wmt[...], preferred_element_type=jnp.float32
            ).astype(jnp.bfloat16)
            for cls in range(4):
                dh, dzp = cls // 2, cls % 2
                for m in range(2):
                    slot = slot_of(dzp + 2 * m, dh)
                    for c in range(2):
                        at = (c * 8 + slot) * ROWS
                        dxb[q, cls, m, c] = part[at : at + ROWS]
            for cls in range(4):

                @pl.when(cls_dest(cls) != x)
                def _():
                    rs_send(cls, q).start()

            @pl.when(q == 1)
            def _():
                for c in range(2):
                    own_x[c].wait()
                    for o in range(1, 4):
                        x_send(o, c).wait_recv()
                        x_hand(o, c).wait_recv()
                wgrad(0, True, False)

            @pl.when(jnp.logical_and(lax.rem(q, 2) == 1, jnp.logical_and(q > 1, q < STEPS - 1)))
            def _():
                wgrad(lax.div(q, 2), False, False)

            @pl.when(q == STEPS - 1)
            def _():
                wgrad(STEPS // 2 - 1, False, True)

        @pl.when(in_range(s, 4))
        def _():
            q = s - 4
            for o in range(3):
                rs_recv(o, q).wait_recv()

            def total(m):
                t = dxb[q, cls_own, m].astype(jnp.float32)
                for o in range(3):
                    t = t + rsb[o, q, m].astype(jnp.float32)
                return t

            ysend[q] = total(1 - keep).astype(jnp.bfloat16)
            y_send(q).start()

        @pl.when(in_range(s, 5))
        def _():
            q = s - 5
            t = dxb[q, cls_own, keep].astype(jnp.float32)
            for o in range(3):
                t = t + rsb[o, q, keep].astype(jnp.float32)
            y_send(q).wait_recv()
            t = (t + yland[q].astype(jnp.float32)).astype(jnp.bfloat16)
            for c in range(2):
                ig_ref[c, q] = t[c]

        return 0

    lax.fori_loop(0, STEPS + 5, step, 0)

    def drain(p, _):
        for kind in (S_ZP, S_ZM, S_Y, S_YZP, S_YZM, S_Y2):
            piece(kind, p).wait_send()
        fwd(p, True).wait_send()
        for g in range(2):
            to_core(g, p).wait_send()
        for cls in range(4):

            @pl.when(cls_dest(cls) != x)
            def _():
                rs_send(cls, p).wait_send()

        y_send(p).wait_send()
        return 0

    lax.fori_loop(0, STEPS, drain, 0)
    for c in range(2):
        for o in range(4):
            x_send(o, c).wait_send()
            if o:
                x_hand(o, c).wait_send()


def write_kernel(acc_ref, ig_ref, wg_ref, ig_out, sems):
    a = pltpu.make_async_copy(acc_ref, wg_ref, sems.at[0])
    b = pltpu.make_async_copy(ig_ref, ig_out, sems.at[1])
    a.start()
    b.start()
    a.wait()
    b.wait()


def local(activations, out_grad, weight, block_mask):
    t_loc, d_loc = activations.shape
    s_loc, f_loc = out_grad.shape
    bf, f32 = jnp.bfloat16, jnp.float32
    dma = pltpu.SemaphoreType.DMA
    hbm = pl.BlockSpec(memory_space=pltpu.HBM)
    vmem = pl.BlockSpec(memory_space=pltpu.VMEM)
    acc, ig = pl.pallas_call(
        comm_kernel,
        out_shape=(
            pltpu.VMEM((d_loc, f_loc), f32),
            pltpu.VMEM((2, STEPS, ROWS, d_loc), bf),
        ),
        in_specs=[hbm, hbm, hbm, vmem],
        out_specs=(vmem, vmem),
        scratch_shapes=[
            pltpu.VMEM((STEPS, 2, 8, ROWS, f_loc), bf),
            pltpu.VMEM((STEPS, 2, 8, ROWS, d_loc), bf),
            pltpu.VMEM((d_loc, 32 * ROWS), bf),
            pltpu.VMEM((d_loc, f_loc), bf),
            pltpu.VMEM((f_loc, d_loc), bf),
            pltpu.VMEM((block_mask.shape[0], f_loc), f32),
            pltpu.VMEM((STEPS, 4, 2, 2, ROWS, d_loc), bf),
            pltpu.VMEM((3, STEPS, 2, 2, ROWS, d_loc), bf),
            pltpu.VMEM((STEPS, 2, ROWS, d_loc), bf),
            pltpu.VMEM((STEPS, 2, ROWS, d_loc), bf),
            dma((7, STEPS)),
            dma((8, STEPS)),
            dma((2, STEPS)),
            dma((2, STEPS)),
            dma((2, 4, 2)),
            dma((2, 4, 2)),
            dma((4, STEPS)),
            dma((3, STEPS)),
            dma((STEPS,)),
            dma((STEPS,)),
            dma((4,)),
        ],
        compiler_params=pltpu.CompilerParams(
            collective_id=0, has_side_effects=True, vmem_limit_bytes=46 * 2**20
        ),
        name="gather_multiply_reduce",
    )(
        activations.reshape(2, STEPS, ROWS, d_loc),
        out_grad.reshape(STEPS, ROWS, f_loc),
        weight,
        block_mask,
    )
    wg, igo = pl.pallas_call(
        write_kernel,
        out_shape=(
            jax.ShapeDtypeStruct((d_loc, f_loc), f32),
            jax.ShapeDtypeStruct((2, STEPS, ROWS, d_loc), bf),
        ),
        in_specs=[vmem, vmem],
        out_specs=(pl.BlockSpec(memory_space=pl.ANY), pl.BlockSpec(memory_space=pl.ANY)),
        scratch_shapes=[dma((2,))],
        compiler_params=pltpu.CompilerParams(vmem_limit_bytes=1 * 2**20),
        name="write_out",
    )(acc, ig)
    return wg, igo.reshape(t_loc, d_loc)


def solution(mesh):
    in_specs = (P("col", "row"), P("row", "col"), P("row", "col"), P("row", "col"))
    out_specs = (P("row", "col"), P("col", "row"))
    return jax.shard_map(local, mesh=mesh, in_specs=in_specs, out_specs=out_specs, check_vma=False)
```

time: 206 us -> 88.6 us (0.43)
  waiting for transfers between devices: 159 us -> 0 us
  Pallas kernels: 0 us -> 86.1 us
  matrix products: 27.7 us -> 0 us
  between operations: 13.8 us -> 0.65 us
  other arithmetic: 4.16 us -> 0 us
    all_gather x2 -> x0, waiting for transfers between devices: 126 us -> none  [the longest x1 99 us: local(): dy_full = lax.all_gather(out_grad, 'row', axis=0, tiled=True)]
    pallas_call x0 -> x2, Pallas kernels: none -> 86.1 us  [the longest x1 83 us: local(): pl.pallas_call(comm_kernel, out_shape=(pltpu.VMEM((d_loc, f_loc), f32), p...]
    reduce_scatter x1 -> x0, waiting for transfers between devices: 30.8 us -> none  [local(): lax.psum_scatter(partial_rounded, 'col', scatter_dimension=0, tiled=True)]
    dot_general x3 -> x0, matrix products: 27.7 us -> none  [the longest x1 13.6 us: local(): lax.dot_general(x_full, dy_full, (((0,), (0,)), ((), ())), preferred_elem...]
    mul x1 -> x0, other arithmetic: 4.14 us -> none  [local(): masked_w = weight * mask_full.astype(jnp.bfloat16)]
  transfers between devices with their start and end apart: 3 -> 0, of which waited for: 3 -> 0; matrix products, arithmetic and copies ran while one was open for 15% -> 0% of each run, Pallas kernels for 0% -> 0%
where the time goes in v1:
time: 88.6 us; the launch traced here: 88.4 us
  Pallas kernels  86.1 us (97%)
  local copies, waits for them, and re-layouts  1.63 us (2%)
    pallas_call x1, Pallas kernels, local(): pl.pallas_call(comm_kernel, out_shape=(pltpu.VMEM((d_loc, f_loc), f32), p...  83 us
    pallas_call x1, Pallas kernels, local(): pl.pallas_call(write_kernel, out_shape=(jax.ShapeDtypeStruct((d_loc, f_lo...  3.14 us

profile of v1, /device:TPU:0, one launch (start us, length us, event | category | flops | bytes accessed | tf_op | source)
XLA Modules:
  0.0 88.4 jit_solution(12929913637434982335)
XLA Ops:
  0.6 0.0 copy-start
  0.6 0.9 %copy-done = bf16[256,512]{1,0:T(8,128)(2,1)S(1)} copy-done((bf16[256,512]{1,0:T(8,128)(2,1)S(1)}, bf16[256,512]{1,0:T(8,128)(2,1)}, u32[]{:S(2)}) %copy-start) | copy-done | bytes 262168
  1.6 0.0 copy-start.1
  1.6 0.7 copy-done.1
  2.3 83.0 %gather_multiply_reduce.1 = (f32[512,3584]{1,0:T(8,128)S(1)}, bf16[2,8,16,512]{3,2,1,0:T(8,128)(2,1)S(1)}) custom-call(bf16[2,8,16,512]{3,2,1,0:T(8,128)(2,1)S(1)} %bitcast.3, bf16[8,16,3584]{2,1,0:T(8,128)(2,1)} %bitcast.4, bf16[512,3584]{1,0:T(8,128)(2,1)} %w_ref.1, s32[8,56]{1,0:T(8,128)S(1)} %copy-done.1), custom_call_target="tpu_custom_call" | custom-call | tf_op jit(solution)/shard_map/gather_multiply_reduce/pallas_call | solution.py:345
  85.2 3.1 %write_out.1 = (f32[512,3584]{1,0:T(8,128)}, bf16[2,8,16,512]{3,2,1,0:T(8,128)(2,1)}) custom-call(f32[512,3584]{1,0:T(8,128)S(1)} %get-tuple-element.6.acc_ref, bf16[2,8,16,512]{3,2,1,0:T(8,128)(2,1)S(1)} %get-tuple-element.7.ig_ref), custom_call_target="tpu_custom_call" | custom-call | tf_op jit(solution)/shard_map/write_out/pallas_call | solution.py:386
Async XLA Ops:
  0.6 1.0 %copy-start = (bf16[256,512]{1,0:T(8,128)(2,1)S(1)}, bf16[256,512]{1,0:T(8,128)(2,1)}, u32[]{:S(2)}) copy-start(bf16[256,512]{1,0:T(8,128)(2,1)} %param.4) | copy-start | bytes 786436
  1.6 0.7 copy-start.1

commit v2 on v1

--- a/solution.py
+++ b/solution.py
@@ -10,22 +10,24 @@
 BLK = 64
 STEPS = 8
 ROWS = 16
-AHEAD = 3
+AHEAD = 2
+LAG_YZ2, LAG_DX = 2, 2
 MESH = pl.DeviceIdType.MESH
 
-M1, OWN, P1, Z2, Y, YP1, YZ2, YM1 = range(8)
+M1, OWN, P1, Y, Z2, YP1, YZ2, YM1 = range(8)
+CORE_GROUPS = ((0, 4), (4, 2), (6, 2))
 S_ZP, S_ZM, S_Y, S_FWD, S_YZP, S_YZM, S_Y2 = range(7)
 
 
 def slot_of(dz, dh):
-    return 4 * dh + (dz + 1 - dh) % 4
+    return ((OWN, P1, Z2, M1), (Y, YP1, YZ2, YM1))[dh][dz]
 
 
 def comm_kernel(
-    x_ref, dy_ref, w_ref, mask_ref,
+    x_ref, dy_ref, w_ref, mask_hbm,
     acc_ref, ig_ref,
-    dyf, xp, xt, wv, wmt, mcols, dxb, rsb, ysend, yland,
-    s_piece, r_piece, s_core, r_core, s_x, r_x, s_rs, r_rs, s_y, r_y, loc,
+    mask_ref, dyf, xp, xt, wv, wmt, mcols, dxb, rsb, ysend, yland,
+    s_piece, r_piece, s_core, r_core, s_x, r_x, s_rs, r_rs, s_half, r_half, s_y, r_y, loc,
 ):
     row, col = lax.axis_index("row"), lax.axis_index("col")
     core = lax.rem(row, 2)
@@ -55,12 +57,16 @@
     own_dy.start()
     w_copy = pltpu.make_async_copy(w_ref, wv, loc.at[1])
     w_copy.start()
+    mask_copy = pltpu.make_async_copy(mask_hbm, mask_ref, loc.at[4])
+    mask_copy.start()
 
     def x_slot(yl_):
         j = yl_ * 4 + x
         dz = lax.rem(lax.div(j, 2) + 4 - z, 4)
         dh = lax.rem(lax.rem(j, 2) + 2 - h, 2)
-        return 4 * dh + lax.rem(dz + 5 - dh, 4)
+        near = lax.rem(dz + 1, 4) + lax.div(dz * (dz - 1) * (3 - dz), 2)
+        far = 3 + dz + lax.div(dz + 2, 3)
+        return near + dh * (far - near)
 
     own_x = [pltpu.make_async_copy(x_ref.at[c], xp.at[:, c, x_slot(yl)], loc.at[2 + c]) for c in range(2)]
     for cp in own_x:
@@ -90,12 +96,12 @@
         return remote(src, dyf.at[p, core, Z2], s_piece.at[S_FWD, p], r_piece.at[Z2, p], zp if up else zm)
 
     def to_core(g, p):
-        lo, n = ((0, 3), (3, 5))[g]
+        lo, n = CORE_GROUPS[g]
         there = dyf.at[p, core, pl.ds(lo, n)]
         return remote(there, there, s_core.at[g, p], r_core.at[g, p], other_core)
 
     def from_core(g, p):
-        lo, n = ((0, 3), (3, 5))[g]
+        lo, n = CORE_GROUPS[g]
         here = dyf.at[p, 1 - core, pl.ds(lo, n)]
         return remote(here, here, s_core.at[g, p], r_core.at[g, p], other_core)
 
@@ -127,6 +133,16 @@
 
     def rs_recv(o, p):
         return remote(rsb.at[o, p], rsb.at[o, p], s_rs.at[0, p], r_rs.at[o, p], xpeer(1))
+
+    def rs_send_half(cls, m, p):
+        xs = cls_dest(cls)
+        o = lax.rem(x + 4 - xs + 3, 4)
+        return remote(
+            dxb.at[p, cls, m], rsb.at[o, p, m], s_half.at[cls, m], r_half.at[o, m], (row, yl * 4 + xs)
+        )
+
+    def rs_recv_half(o, m, p):
+        return remote(rsb.at[o, p, m], rsb.at[o, p, m], s_half.at[0, 0], r_half.at[o, m], xpeer(1))
 
     def y_send(p):
         return remote(ysend.at[p], yland.at[p], s_y.at[p], r_y.at[p], yn)
@@ -141,6 +157,7 @@
     nbr, nbc = mask_ref.shape
     tile = 512
     n_tiles = f_loc // tile
+    mask_copy.wait()
     mask_bf = mask_ref[...].astype(jnp.bfloat16)
 
     def spread(i, _):
@@ -168,9 +185,10 @@
     lax.fori_loop(0, n_tiles, mask_w, 0)
     own_dy.wait()
 
-    def wgrad(b, first, last):
+    def wgrad(b, first, last, lo=0, hi=n_tiles):
         span = xt.shape[1]
-        xt[...] = xp[pl.ds(2 * b, 2)].reshape(span, d_loc).T
+        if lo == 0:
+            xt[...] = xp[pl.ds(2 * b, 2)].reshape(span, d_loc).T
 
         def one(i, _):
             cols = pl.ds(pl.multiple_of(i * tile, tile), tile)
@@ -186,33 +204,100 @@
                 acc_ref[:, cols] = part
             return 0
 
-        lax.fori_loop(0, n_tiles, one, 0)
-
-    def in_range(s, lag):
-        return jnp.logical_and(s >= lag, s < STEPS + lag)
+        lax.fori_loop(lo, hi, one, 0)
+
+    def dx_rows(q, lo, n):
+        part = jnp.dot(
+            dyf[q, :, lo : lo + n].reshape(2 * n * ROWS, f_loc), wmt[...], preferred_element_type=jnp.float32
+        ).astype(jnp.bfloat16)
+        for cls in range(4):
+            dh, dzp = cls // 2, cls % 2
+            for m in range(2):
+                slot = slot_of(dzp + 2 * m, dh)
+                if not lo <= slot < lo + n:
+                    continue
+                for c in range(2):
+                    at = (c * n + slot - lo) * ROWS
+                    dxb[q, cls, m, c] = part[at : at + ROWS]
+                if n < 8:
+
+                    @pl.when(cls_dest(cls) != x)
+                    def _():
+                        rs_send_half(cls, m, q).start()
+
+    def dx_step(q):
+        for g in range(3):
+            from_core(g, q).wait_recv()
+        dx_rows(q, 0, 8)
+        for cls in range(4):
+
+            @pl.when(cls_dest(cls) != x)
+            def _():
+                rs_send(cls, q).start()
+
+    def rs_total(q, m):
+        t = dxb[q, cls_own, m].astype(jnp.float32)
+        for o in range(3):
+            t = t + rsb[o, q, m].astype(jnp.float32)
+        return t
+
+    def rs_wait(q, m):
+        for o in range(3):
+            if isinstance(q, int) and q == STEPS - 1:
+                rs_recv_half(o, m, q).wait_recv()
+            else:
+                rs_recv(o, q).wait_recv()
+
+    def rs_along_y(q):
+        rs_wait(q, 1 - keep)
+        ysend[q] = rs_total(q, 1 - keep).astype(jnp.bfloat16)
+        y_send(q).start()
+
+    def rs_finish(q):
+        if isinstance(q, int) and q == STEPS - 1:
+            rs_wait(q, keep)
+        t = rs_total(q, keep)
+        y_send(q).wait_recv()
+        t = (t + yland[q].astype(jnp.float32)).astype(jnp.bfloat16)
+        for c in range(2):
+            ig_ref[c, q] = t[c]
+
+    def neighbours(p, more):
+        piece(S_ZP, p).wait_recv()
+        piece(S_ZM, p).wait_recv()
+
+        @pl.when(lax.rem(p, 2) == 0)
+        def _():
+            fwd(p, True).start()
+
+        @pl.when(lax.rem(p, 2) == 1)
+        def _():
+            fwd(p, False).start()
+
+        piece(S_Y, p).wait_recv()
+        piece(S_YZP, p).start()
+        piece(S_YZM, p).start()
+        to_core(0, p).start()
+
+        @pl.when(more)
+        def _():
+            own_sends(p + AHEAD)
+
+    def second(p):
+        fwd(p, True).wait_recv()
+        piece(S_Y2, p).start()
+
+    def second_core(p):
+        piece(S_YZM, p).wait_recv()
+        to_core(1, p).start()
+
+    def third(p):
+        piece(S_YZP, p).wait_recv()
+        piece(S_Y2, p).wait_recv()
+        to_core(2, p).start()
 
     def step(s, _):
-        @pl.when(s < STEPS)
-        def _():
-            piece(S_ZP, s).wait_recv()
-            piece(S_ZM, s).wait_recv()
-
-            @pl.when(s < STEPS - AHEAD)
-            def _():
-                own_sends(s + AHEAD)
-
-            @pl.when(lax.rem(s, 2) == 0)
-            def _():
-                fwd(s, True).start()
-
-            @pl.when(lax.rem(s, 2) == 1)
-            def _():
-                fwd(s, False).start()
-
-            to_core(0, s).start()
-            piece(S_Y, s).wait_recv()
-            piece(S_YZP, s).start()
-            piece(S_YZM, s).start()
+        neighbours(s, s < STEPS - AHEAD)
 
         @pl.when(s == 0)
         def _():
@@ -221,104 +306,101 @@
                 for o in range(1, 4):
                     x_hand(o, c).start()
 
-        @pl.when(in_range(s, 1))
-        def _():
-            q = s - 1
-            fwd(q, True).wait_recv()
-            piece(S_Y2, q).start()
-            piece(S_YZP, q).wait_recv()
-            piece(S_YZM, q).wait_recv()
-
-        @pl.when(in_range(s, 2))
-        def _():
-            q = s - 2
-            piece(S_Y2, q).wait_recv()
-            to_core(1, q).start()
-
-        @pl.when(in_range(s, 3))
-        def _():
-            q = s - 3
-            from_core(0, q).wait_recv()
-            from_core(1, q).wait_recv()
-            part = jnp.dot(
-                dyf[q].reshape(16 * ROWS, f_loc), wmt[...], preferred_element_type=jnp.float32
-            ).astype(jnp.bfloat16)
-            for cls in range(4):
-                dh, dzp = cls // 2, cls % 2
-                for m in range(2):
-                    slot = slot_of(dzp + 2 * m, dh)
-                    for c in range(2):
-                        at = (c * 8 + slot) * ROWS
-                        dxb[q, cls, m, c] = part[at : at + ROWS]
-            for cls in range(4):
-
-                @pl.when(cls_dest(cls) != x)
-                def _():
-                    rs_send(cls, q).start()
-
-            @pl.when(q == 1)
+        @pl.when(s >= LAG_YZ2)
+        def _():
+            third(s - LAG_YZ2)
+
+        @pl.when(s >= 1)
+        def _():
+            second(s - 1)
+            second_core(s - 1)
+
+        @pl.when(s >= LAG_DX)
+        def _():
+            q = s - LAG_DX
+            dx_step(q)
+
+            @pl.when(q == 2)
             def _():
                 for c in range(2):
                     own_x[c].wait()
                     for o in range(1, 4):
                         x_send(o, c).wait_recv()
                         x_hand(o, c).wait_recv()
-                wgrad(0, True, False)
-
-            @pl.when(jnp.logical_and(lax.rem(q, 2) == 1, jnp.logical_and(q > 1, q < STEPS - 1)))
-            def _():
-                wgrad(lax.div(q, 2), False, False)
-
-            @pl.when(q == STEPS - 1)
-            def _():
-                wgrad(STEPS // 2 - 1, False, True)
-
-        @pl.when(in_range(s, 4))
-        def _():
-            q = s - 4
-            for o in range(3):
-                rs_recv(o, q).wait_recv()
-
-            def total(m):
-                t = dxb[q, cls_own, m].astype(jnp.float32)
-                for o in range(3):
-                    t = t + rsb[o, q, m].astype(jnp.float32)
-                return t
-
-            ysend[q] = total(1 - keep).astype(jnp.bfloat16)
-            y_send(q).start()
-
-        @pl.when(in_range(s, 5))
-        def _():
-            q = s - 5
-            t = dxb[q, cls_own, keep].astype(jnp.float32)
-            for o in range(3):
-                t = t + rsb[o, q, keep].astype(jnp.float32)
-            y_send(q).wait_recv()
-            t = (t + yland[q].astype(jnp.float32)).astype(jnp.bfloat16)
-            for c in range(2):
-                ig_ref[c, q] = t[c]
+                wgrad(0, True, False, 0, 4)
+
+            @pl.when(q == 3)
+            def _():
+                wgrad(0, True, False, 4, n_tiles)
+
+            @pl.when(q == 4)
+            def _():
+                wgrad(1, False, False, 0, 4)
+
+            @pl.when(q == 5)
+            def _():
+                wgrad(1, False, False, 4, n_tiles)
+
+        @pl.when(s >= LAG_DX + 1)
+        def _():
+            rs_along_y(s - LAG_DX - 1)
+
+        @pl.when(s >= LAG_DX + 2)
+        def _():
+            rs_finish(s - LAG_DX - 2)
 
         return 0
 
-    lax.fori_loop(0, STEPS + 5, step, 0)
+    lax.fori_loop(0, STEPS, step, 0)
+    last = STEPS - 1
+    third(last - 1)
+    second(last)
+    second_core(last)
+    from_core(0, last).wait_recv()
+    dx_rows(last, 0, 4)
+    dx_step(last - 1)
+    rs_along_y(last - 2)
+    rs_finish(last - 3)
+    third(last)
+    wgrad(2, False, False, 0, 3)
+    from_core(1, last).wait_recv()
+    from_core(2, last).wait_recv()
+    dx_rows(last, 4, 4)
+    rs_along_y(last - 1)
+    rs_finish(last - 2)
+    wgrad(2, False, False, 3, n_tiles)
+    rs_along_y(last)
+    rs_finish(last - 1)
+    wgrad(3, False, True)
+    rs_finish(last)
 
     def drain(p, _):
         for kind in (S_ZP, S_ZM, S_Y, S_YZP, S_YZM, S_Y2):
             piece(kind, p).wait_send()
         fwd(p, True).wait_send()
-        for g in range(2):
+        for g in range(3):
             to_core(g, p).wait_send()
-        for cls in range(4):
-
-            @pl.when(cls_dest(cls) != x)
-            def _():
-                rs_send(cls, p).wait_send()
-
         y_send(p).wait_send()
         return 0
 
+    def drain_rs(p, _):
+        for cls in range(4):
+
+            @pl.when(cls_dest(cls) != x)
+            def _():
+                rs_send(cls, p).wait_send()
+
+        return 0
+
     lax.fori_loop(0, STEPS, drain, 0)
+    lax.fori_loop(0, STEPS - 1, drain_rs, 0)
+    for cls in range(4):
+
+        @pl.when(cls_dest(cls) != x)
+        def _():
+            for m in range(2):
+                rs_send_half(cls, m, STEPS - 1).wait_send()
+
     for c in range(2):
         for o in range(4):
             x_send(o, c).wait_send()
@@ -327,12 +409,16 @@
 
 
 def write_kernel(acc_ref, ig_ref, wg_ref, ig_out, sems):
-    a = pltpu.make_async_copy(acc_ref, wg_ref, sems.at[0])
-    b = pltpu.make_async_copy(ig_ref, ig_out, sems.at[1])
-    a.start()
-    b.start()
-    a.wait()
-    b.wait()
+    parts = 8
+    rows = acc_ref.shape[0] // parts
+    copies = [pltpu.make_async_copy(ig_ref, ig_out, sems.at[parts])]
+    for i in range(parts):
+        part = pl.ds(i * rows, rows)
+        copies.append(pltpu.make_async_copy(acc_ref.at[part], wg_ref.at[part], sems.at[i]))
+    for cp in copies:
+        cp.start()
+    for cp in copies:
+        cp.wait()
 
 
 def local(activations, out_grad, weight, block_mask):
@@ -348,9 +434,10 @@
             pltpu.VMEM((d_loc, f_loc), f32),
             pltpu.VMEM((2, STEPS, ROWS, d_loc), bf),
         ),
-        in_specs=[hbm, hbm, hbm, vmem],
+        in_specs=[hbm] * 4,
         out_specs=(vmem, vmem),
         scratch_shapes=[
+            pltpu.VMEM(block_mask.shape, jnp.int32),
             pltpu.VMEM((STEPS, 2, 8, ROWS, f_loc), bf),
             pltpu.VMEM((STEPS, 2, 8, ROWS, d_loc), bf),
             pltpu.VMEM((d_loc, 32 * ROWS), bf),
@@ -363,25 +450,32 @@
             pltpu.VMEM((STEPS, 2, ROWS, d_loc), bf),
             dma((7, STEPS)),
             dma((8, STEPS)),
-            dma((2, STEPS)),
-            dma((2, STEPS)),
+            dma((3, STEPS)),
+            dma((3, STEPS)),
             dma((2, 4, 2)),
             dma((2, 4, 2)),
             dma((4, STEPS)),
             dma((3, STEPS)),
+            dma((4, 2)),
+            dma((3, 2)),
             dma((STEPS,)),
             dma((STEPS,)),
-            dma((4,)),
+            dma((5,)),
         ],
         compiler_params=pltpu.CompilerParams(
             collective_id=0, has_side_effects=True, vmem_limit_bytes=46 * 2**20
         ),
         name="gather_multiply_reduce",
     )(
-        activations.reshape(2, STEPS, ROWS, d_loc),
-        out_grad.reshape(STEPS, ROWS, f_loc),
-        weight,
-        block_mask,
+        *(
+            pltpu.with_memory_space_constraint(a, pltpu.HBM)
+            for a in (
+                activations.reshape(2, STEPS, ROWS, d_loc),
+                out_grad.reshape(STEPS, ROWS, f_loc),
+                weight,
+                block_mask,
+            )
+        )
     )
     wg, igo = pl.pallas_call(
         write_kernel,
@@ -391,7 +485,7 @@
         ),
         in_specs=[vmem, vmem],
         out_specs=(pl.BlockSpec(memory_space=pl.ANY), pl.BlockSpec(memory_space=pl.ANY)),
-        scratch_shapes=[dma((2,))],
+        scratch_shapes=[dma((9,))],
         compiler_params=pltpu.CompilerParams(vmem_limit_bytes=1 * 2**20),
         name="write_out",
     )(acc, ig)

time: 88.6 us -> 82.5 us (0.931)
  Pallas kernels: 86.1 us -> 81.7 us
  local copies, waits for them, and re-layouts: 1.63 us -> 0 us
    pallas_call x1, Pallas kernels: 83 us -> 78.6 us  [local(): pl.pallas_call(comm_kernel, out_shape=(pltpu.VMEM((d_loc, f_loc), f32), p...]
    unnamed x4 -> x0, local copies, waits for them, and re-layouts: 1.63 us -> none
where the time goes in v2:
time: 82.5 us; the launch traced here: 82.4 us
  Pallas kernels  81.7 us (99%)
    pallas_call x1, Pallas kernels, local(): pl.pallas_call(comm_kernel, out_shape=(pltpu.VMEM((d_loc, f_loc), f32), p...  78.6 us
    pallas_call x1, Pallas kernels, local(): pl.pallas_call(write_kernel, out_shape=(jax.ShapeDtypeStruct((d_loc, f_lo...  3.15 us

profile of v2, /device:TPU:0, one launch (start us, length us, event | category | flops | bytes accessed | tf_op | source)
XLA Modules:
  0.0 82.4 jit_solution(11492549446697073436)
XLA Ops:
  0.6 78.6 %gather_multiply_reduce.1 = (f32[512,3584]{1,0:T(8,128)S(1)}, bf16[2,8,16,512]{3,2,1,0:T(8,128)(2,1)S(1)}) custom-call(bf16[2,8,16,512]{3,2,1,0:T(8,128)(2,1)} %bitcast.4, bf16[8,16,3584]{2,1,0:T(8,128)(2,1)} %bitcast.3, bf16[512,3584]{1,0:T(8,128)(2,1)} %w_ref.1, s32[8,56]{1,0:T(8,128)} %mask_hbm.1), custom_call_target="tpu_custom_call" | custom-call | tf_op jit(solution)/shard_map/gather_multiply_reduce/pallas_call | solution.py:431
  79.2 3.1 %write_out.1 = (f32[512,3584]{1,0:T(8,128)}, bf16[2,8,16,512]{3,2,1,0:T(8,128)(2,1)}) custom-call(f32[512,3584]{1,0:T(8,128)S(1)} %get-tuple-element.6.acc_ref, bf16[2,8,16,512]{3,2,1,0:T(8,128)(2,1)S(1)} %get-tuple-element.7.ig_ref), custom_call_target="tpu_custom_call" | custom-call | tf_op jit(solution)/shard_map/write_out/pallas_call | solution.py:480

commit v3 on v2

--- a/solution.py
+++ b/solution.py
@@ -11,7 +11,7 @@
 STEPS = 8
 ROWS = 16
 AHEAD = 2
-LAG_YZ2, LAG_DX = 2, 2
+LAG_YZ2, LAG_DX, LAG_SUM = 2, 2, 5
 MESH = pl.DeviceIdType.MESH
 
 M1, OWN, P1, Y, Z2, YP1, YZ2, YM1 = range(8)
@@ -185,14 +185,15 @@
     lax.fori_loop(0, n_tiles, mask_w, 0)
     own_dy.wait()
 
-    def wgrad(b, first, last, lo=0, hi=n_tiles):
+    def wgrad(b, first, last, lo=0, hi=2):
+        wide = f_loc // 2
         span = xt.shape[1]
         if lo == 0:
             xt[...] = xp[pl.ds(2 * b, 2)].reshape(span, d_loc).T
 
         def one(i, _):
-            cols = pl.ds(pl.multiple_of(i * tile, tile), tile)
-            dy2 = dyf[pl.ds(2 * b, 2), :, :, :, cols].reshape(span, tile)
+            cols = pl.ds(pl.multiple_of(i * wide, wide), wide)
+            dy2 = dyf[pl.ds(2 * b, 2), :, :, :, cols].reshape(span, wide)
             part = jnp.dot(xt[...], dy2, preferred_element_type=jnp.float32)
             if not first:
                 part = part + acc_ref[:, cols]
@@ -327,51 +328,46 @@
                     for o in range(1, 4):
                         x_send(o, c).wait_recv()
                         x_hand(o, c).wait_recv()
-                wgrad(0, True, False, 0, 4)
+                wgrad(0, True, False)
 
             @pl.when(q == 3)
             def _():
-                wgrad(0, True, False, 4, n_tiles)
+                wgrad(1, False, False, 0, 1)
 
             @pl.when(q == 4)
             def _():
-                wgrad(1, False, False, 0, 4)
-
-            @pl.when(q == 5)
-            def _():
-                wgrad(1, False, False, 4, n_tiles)
-
-        @pl.when(s >= LAG_DX + 1)
-        def _():
-            rs_along_y(s - LAG_DX - 1)
-
-        @pl.when(s >= LAG_DX + 2)
-        def _():
-            rs_finish(s - LAG_DX - 2)
+                wgrad(1, False, False, 1, 2)
+
+        @pl.when(s >= LAG_SUM)
+        def _():
+            rs_along_y(s - LAG_SUM)
 
         return 0
 
     lax.fori_loop(0, STEPS, step, 0)
     last = STEPS - 1
+    wgrad(2, False, False)
     third(last - 1)
     second(last)
     second_core(last)
+    dx_step(last - 1)
     from_core(0, last).wait_recv()
     dx_rows(last, 0, 4)
-    dx_step(last - 1)
-    rs_along_y(last - 2)
-    rs_finish(last - 3)
     third(last)
-    wgrad(2, False, False, 0, 3)
+    for q in range(STEPS - LAG_SUM, last - 1):
+        rs_along_y(q)
+    for q in range(STEPS - LAG_SUM):
+        rs_finish(q)
     from_core(1, last).wait_recv()
     from_core(2, last).wait_recv()
     dx_rows(last, 4, 4)
     rs_along_y(last - 1)
-    rs_finish(last - 2)
-    wgrad(2, False, False, 3, n_tiles)
+    for q in range(STEPS - LAG_SUM, last - 1):
+        rs_finish(q)
+    wgrad(3, False, True, 0, 1)
     rs_along_y(last)
     rs_finish(last - 1)
-    wgrad(3, False, True)
+    wgrad(3, False, True, 1, 2)
     rs_finish(last)
 
     def drain(p, _):

time: 82.5 us -> 80.8 us (0.979); the launches traced: 82.4 us -> 79.8 us
  Pallas kernels: 81.7 us -> 79.1 us
    pallas_call x1, Pallas kernels: 78.6 us -> 76 us  [local(): pl.pallas_call(comm_kernel, out_shape=(pltpu.VMEM((d_loc, f_loc), f32), p...]
where the time goes in v3:
time: 80.8 us; the launch traced here: 79.8 us
  Pallas kernels  79.1 us (98%)
    pallas_call x1, Pallas kernels, local(): pl.pallas_call(comm_kernel, out_shape=(pltpu.VMEM((d_loc, f_loc), f32), p...  76 us
    pallas_call x1, Pallas kernels, local(): pl.pallas_call(write_kernel, out_shape=(jax.ShapeDtypeStruct((d_loc, f_lo...  3.15 us

profile of v3, /device:TPU:0, one launch (start us, length us, event | category | flops | bytes accessed | tf_op | source)
XLA Modules:
  0.0 79.8 jit_solution(17497759141543284753)
XLA Ops:
  0.6 76.0 %gather_multiply_reduce.1 = (f32[512,3584]{1,0:T(8,128)S(1)}, bf16[2,8,16,512]{3,2,1,0:T(8,128)(2,1)S(1)}) custom-call(bf16[2,8,16,512]{3,2,1,0:T(8,128)(2,1)} %bitcast.4, bf16[8,16,3584]{2,1,0:T(8,128)(2,1)} %bitcast.3, bf16[512,3584]{1,0:T(8,128)(2,1)} %w_ref.1, s32[8,56]{1,0:T(8,128)} %mask_hbm.1), custom_call_target="tpu_custom_call" | custom-call | tf_op jit(solution)/shard_map/gather_multiply_reduce/pallas_call | solution.py:427
  76.6 3.1 %write_out.1 = (f32[512,3584]{1,0:T(8,128)}, bf16[2,8,16,512]{3,2,1,0:T(8,128)(2,1)}) custom-call(f32[512,3584]{1,0:T(8,128)S(1)} %get-tuple-element.6.acc_ref, bf16[2,8,16,512]{3,2,1,0:T(8,128)(2,1)S(1)} %get-tuple-element.7.ig_ref), custom_call_target="tpu_custom_call" | custom-call | tf_op jit(solution)/shard_map/write_out/pallas_call | solution.py:476

commit v4 on v3

--- a/solution.py
+++ b/solution.py
@@ -300,21 +300,21 @@
     def step(s, _):
         neighbours(s, s < STEPS - AHEAD)
 
-        @pl.when(s == 0)
+        @pl.when(s >= LAG_YZ2)
+        def _():
+            third(s - LAG_YZ2)
+
+        @pl.when(s >= 1)
+        def _():
+            second(s - 1)
+            second_core(s - 1)
+
+        @pl.when(s == 1)
         def _():
             for c in range(2):
                 x_send(0, c).wait_recv()
                 for o in range(1, 4):
                     x_hand(o, c).start()
-
-        @pl.when(s >= LAG_YZ2)
-        def _():
-            third(s - LAG_YZ2)
-
-        @pl.when(s >= 1)
-        def _():
-            second(s - 1)
-            second_core(s - 1)
 
         @pl.when(s >= LAG_DX)
         def _():

time: 80.8 us -> 81 us (level)
  no operation moved by 1% of the time
where the time goes in v4:
time: 81 us; the launch traced here: 80 us
  Pallas kernels  79.4 us (98%)
    pallas_call x1, Pallas kernels, local(): pl.pallas_call(comm_kernel, out_shape=(pltpu.VMEM((d_loc, f_loc), f32), p...  76.3 us
    pallas_call x1, Pallas kernels, local(): pl.pallas_call(write_kernel, out_shape=(jax.ShapeDtypeStruct((d_loc, f_lo...  3.15 us

profile of v4, /device:TPU:0, one launch (start us, length us, event | category | flops | bytes accessed | tf_op | source)
XLA Modules:
  0.0 80.0 jit_solution(4437497327482561858)
XLA Ops:
  0.6 76.3 %gather_multiply_reduce.1 = (f32[512,3584]{1,0:T(8,128)S(1)}, bf16[2,8,16,512]{3,2,1,0:T(8,128)(2,1)S(1)}) custom-call(bf16[2,8,16,512]{3,2,1,0:T(8,128)(2,1)} %bitcast.4, bf16[8,16,3584]{2,1,0:T(8,128)(2,1)} %bitcast.3, bf16[512,3584]{1,0:T(8,128)(2,1)} %w_ref.1, s32[8,56]{1,0:T(8,128)} %mask_hbm.1), custom_call_target="tpu_custom_call" | custom-call | tf_op jit(solution)/shard_map/gather_multiply_reduce/pallas_call | solution.py:427
  76.9 3.1 %write_out.1 = (f32[512,3584]{1,0:T(8,128)}, bf16[2,8,16,512]{3,2,1,0:T(8,128)(2,1)}) custom-call(f32[512,3584]{1,0:T(8,128)S(1)} %get-tuple-element.6.acc_ref, bf16[2,8,16,512]{3,2,1,0:T(8,128)(2,1)S(1)} %get-tuple-element.7.ig_ref), custom_call_target="tpu_custom_call" | custom-call | tf_op jit(solution)/shard_map/write_out/pallas_call | solution.py:476
